TPU v7x, 32 devices: a whole 2x2x4 slice. The times are simulated.
32 devices in a mesh: row: 8 (over z, core), col: 4 (over y, x).
Axes of the slice: x: 2, y: 2, z: 4, core: 2. Of those that a mesh axis runs over, the one named last changes fastest.
Arguments:
- features: bfloat16 [16384, 256], P(('row', 'col')), may hold values from -6 to 6
- blocks: bfloat16 [8, 4, 192, 64, 64], P('row', 'col'), may hold values from -0.3125 to 0.3125
- block_rows: int32 [8, 4, 192], P('row', 'col'), may hold values from 0 to 31
- block_cols: int32 [8, 4, 192], P('row', 'col'), may hold values from 0 to 63
- block_count: int32 [8, 4], P('row', 'col'), may hold values from 1 to 192, as said below
- w_in: bfloat16 [512, 1024], replicated, may hold values from -0.25 to 0.25
- w_mid: bfloat16 [1024, 1024], replicated, may hold values from -0.1875 to 0.1875
- w_out: bfloat16 [1024, 256], replicated, may hold values from -0.1875 to 0.1875
- cotangent: bfloat16 [16384, 256], P(('row', 'col')), may hold values from -6 to 6
Outputs:
- updated: bfloat16 [16384, 256], P(('row', 'col'))
- grad_nodes: bfloat16 [16384, 256], P(('row', 'col'))
- grad_in: float32 [512, 1024], replicated
- grad_mid: float32 [1024, 1024], replicated
- grad_out: float32 [1024, 256], replicated
Inputs may be any that keep to these rules, and one draw needn't show every extreme that they name: Only slots below a cell's block_count are used; the busiest cell uses all 192 slots.
All inputs are finite; a program needn't handle non-finite values.
Results may differ from a plain program's by a relative error of at most 0.015.
Values may be sent and summed in bfloat16 or wider, within the bound.
A program may use at most 128 MiB of HBM per device.

v0:
```python
import math

import jax
import jax.numpy as jnp
from jax import lax
from jax.sharding import PartitionSpec as P


def silu_grad(value):
    sig = jax.nn.sigmoid(value)
    return sig * (1.0 + value * (1.0 - sig))


def cell_term(cell_blocks, gather_idx, add_idx, count, source, n_dst, transposed):
    slots = cell_blocks.shape[0]
    side = cell_blocks.shape[1]
    n_src = source.shape[0]
    feats = source.shape[2]
    width = slots // 8
    form = "sba,sbf->saf" if transposed else "sab,sbf->saf"
    flat_source = source.reshape(n_src, side * feats)
    src_ids = jnp.arange(n_src, dtype=jnp.int32)
    dst_ids = jnp.arange(n_dst, dtype=jnp.int32)

    def one_group(step, total):
        start = step * width
        part_blocks = lax.dynamic_slice_in_dim(cell_blocks, start, width, 0)
        part_gather = lax.dynamic_slice_in_dim(gather_idx, start, width, 0)
        part_add = lax.dynamic_slice_in_dim(add_idx, start, width, 0)
        pick_table = (part_gather[:, None] == src_ids[None, :]).astype(jnp.bfloat16)
        picked = jnp.dot(pick_table, flat_source, preferred_element_type=jnp.float32).astype(
            jnp.bfloat16
        )
        picked = picked.reshape(width, side, feats)
        prod = jnp.einsum(form, part_blocks, picked, preferred_element_type=jnp.float32)
        prod = prod.reshape(width, side * feats)
        upper = prod.astype(jnp.bfloat16)
        lower = (prod - upper.astype(jnp.float32)).astype(jnp.bfloat16)
        live = start + jnp.arange(width, dtype=jnp.int32) < count
        add_table = ((part_add[:, None] == dst_ids[None, :]) & live[:, None]).astype(jnp.bfloat16)
        total = total + jnp.einsum(
            "sn,sk->nk", add_table, upper, preferred_element_type=jnp.float32
        )
        return total + jnp.einsum("sn,sk->nk", add_table, lower, preferred_element_type=jnp.float32)

    steps = 8
    total = lax.fori_loop(0, steps, one_group, jnp.zeros((n_dst, side * feats), jnp.float32))
    return total.reshape(n_dst * side, feats)


def shards(features, blocks, block_rows, block_cols, block_count, w_in, w_mid, w_out, cotangent):
    side = blocks.shape[-1]
    feats = features.shape[1]
    node_dev = features.shape[0]
    cell_blocks = blocks[0, 0]
    rows_here = block_rows[0, 0]
    cols_here = block_cols[0, 0]
    count = block_count[0, 0]
    row_blocks = node_dev * lax.axis_size("col") // side
    column_feats = lax.all_gather(features, "row", axis=0, tiled=True)
    col_blocks = column_feats.shape[0] // side
    partial_value = cell_term(
        cell_blocks,
        cols_here,
        rows_here,
        count,
        column_feats.reshape(col_blocks, side, feats),
        row_blocks,
        False,
    )
    aggregated = lax.psum_scatter(
        partial_value.astype(jnp.bfloat16), "col", scatter_dimension=0, tiled=True
    )
    joined = jnp.concatenate([features, aggregated], axis=1)
    pre_one = jnp.dot(joined, w_in, preferred_element_type=jnp.float32)
    act_one = jax.nn.silu(pre_one).astype(jnp.bfloat16)
    pre_two = jnp.dot(act_one, w_mid, preferred_element_type=jnp.float32)
    act_two = jax.nn.silu(pre_two).astype(jnp.bfloat16)
    updated = (
        features.astype(jnp.float32) + jnp.dot(act_two, w_out, preferred_element_type=jnp.float32)
    ).astype(jnp.bfloat16)
    ratio = 1.0 / math.sqrt(node_dev * lax.axis_size("row") * lax.axis_size("col"))
    local_out = jnp.einsum("nh,nf->hf", act_two, cotangent, preferred_element_type=jnp.float32)
    grad_pre_two = (
        jnp.dot(cotangent, w_out.T, preferred_element_type=jnp.float32) * silu_grad(pre_two)
    ).astype(jnp.bfloat16)
    local_mid = jnp.einsum("nh,nk->hk", act_one, grad_pre_two, preferred_element_type=jnp.float32)
    grad_pre_one = (
        jnp.dot(grad_pre_two, w_mid.T, preferred_element_type=jnp.float32) * silu_grad(pre_one)
    ).astype(jnp.bfloat16)
    local_in = jnp.einsum("nd,nh->dh", joined, grad_pre_one, preferred_element_type=jnp.float32)
    grad_joined = jnp.dot(grad_pre_one, w_in.T, preferred_element_type=jnp.float32)
    direct = cotangent.astype(jnp.float32) + grad_joined[:, :feats]
    grad_agg = grad_joined[:, feats:].astype(jnp.bfloat16)
    row_grads = lax.all_gather(grad_agg, "col", axis=0, tiled=True)
    back = cell_term(
        cell_blocks,
        rows_here,
        cols_here,
        count,
        row_grads.reshape(row_blocks, side, feats),
        col_blocks,
        True,
    )
    relaid = lax.psum_scatter(
        back.astype(jnp.bfloat16), "row", scatter_dimension=0, tiled=True
    ).astype(jnp.float32)
    grad_nodes = (direct + relaid).astype(jnp.bfloat16)
    summed_in, summed_mid, summed_out = lax.psum((local_in, local_mid, local_out), ("row", "col"))
    return (updated, grad_nodes, summed_in * ratio, summed_mid * ratio, summed_out * ratio)


def solution(mesh):
    placed = (
        P(("row", "col"), None),
        P("row", "col", None, None, None),
        P("row", "col", None),
        P("row", "col", None),
        P("row", "col"),
        P(),
        P(),
        P(),
        P(("row", "col"), None),
    )
    return jax.shard_map(
        shards,
        mesh=mesh,
        in_specs=placed,
        out_specs=(P(("row", "col"), None), P(("row", "col"), None), P(), P(), P()),
        check_vma=False,
    )
```

profile of v0, /device:TPU:0, one launch (start us, length us, event | category | flops | bytes accessed | tf_op | source)
XLA Modules:
  0.0 397.7 jit_solution(2176733292544460156)
XLA Ops:
  8.0 5.1 %copy.15 = bf16[192,64,64]{2,1,0:T(8,128)(2,1)} copy(bf16[192,64,64]{0,2,1:T(8,128)(2,1)} %bitcast.67) | data formatting | bytes 3145728
  13.1 28.4 %all-gather.3.cloned.1.call-done = bf16[4096,256]{1,0:T(8,128)(2,1)} async-done(((bf16[512,256]{1,0:T(8,128)(2,1)}), bf16[4096,256]{1,0:T(8,128)(2,1)}) %all-gather.3.cloned.1.call-update) | async-done | bytes 2097168 | tf_op jit(solution)/shard_map/all_gather | solution.py:60
  41.5 4.2 %reshape_reshape.6 = bf16[64,16384]{1,0:T(8,128)(2,1)} reshape(bf16[4096,256]{1,0:T(8,128)(2,1)} %all-gather.3.cloned.1.call-done) | data formatting | bytes 4194304 | tf_op jit(solution)/shard_map/reshape;reshape | solution.py:21
  45.7 62.5 %while.28 = (s32[]{:T(128)}, f32[32,16384]{1,0:T(8,128)}, s32[192]{0:T(256)S(1)}, s32[]{:T(128)}, bf16[192,64,64]{2,1,0:T(8,128)(2,1)}, /*index=5*/s32[192]{0:T(...) while((s32[]{:T(128)}, f32[32,16384]{1,0:T(8,128)}, ...), condition=%wide.region_1.0_spmd.clone, body=%wide.region_0.0_spmd.clone.sunk | while | flops 154931776 | bytes 30278596 | solution.py:47
  45.7 2.0 convolution_convert_fusion.4
  53.5 2.0 convolution_convert_fusion.4
  69.2 2.0 convolution_convert_fusion.4
  77.0 2.0 convolution_convert_fusion.4
  84.8 2.0 convolution_convert_fusion.4
  92.6 2.0 convolution_convert_fusion.4
  100.4 2.0 convolution_convert_fusion.4
  111.3 27.2 %reduce-scatter.3.cloned.1.call-done = bf16[512,256]{1,0:T(8,128)(2,1)} async-done(((bf16[2048,256]{1,0:T(8,128)(2,1)}), bf16[512,256]{1,0:T(8,128)(2,1)}) %reduce-scatter.3.cloned.1.call-update) | async-done | bytes 262160 | tf_op jit(solution)/shard_map/reduce_scatter | solution.py:71
  141.4 2.6 multiply_convert_fusion.2
  149.6 5.1 %copy.14 = bf16[1,1,192,64,64]{3,4,2,1,0:T(8,128)(2,1)} copy(bf16[1,1,192,64,64]{2,4,3,1,0:T(8,128)(2,1)S(1)} %copy-done.4) | data formatting | bytes 3145728 | tf_op args[1]
  154.8 2.8 fusion.42
  159.9 3.4 fusion.37
  163.4 12.8 %all-gather.5.cloned.1.call-done = bf16[2048,256]{1,0:T(8,128)(2,1)} async-done(((bf16[512,256]{1,0:T(8,128)(2,1)}), bf16[2048,256]{1,0:T(8,128)(2,1)}) %all-gather.5.cloned.1.call-update) | async-done | bytes 1048592 | tf_op jit(solution)/shard_map/all_gather | solution.py:95
  177.7 60.7 %while.29 = (s32[]{:T(128)}, f32[64,16384]{1,0:T(8,128)}, s32[192]{0:T(256)S(1)}, s32[]{:T(128)}, bf16[192,64,64]{1,2,0:T(8,128)(2,1)}, /*index=5*/s32[192]{0:T(...) while((s32[]{:T(128)}, f32[64,16384]{1,0:T(8,128)}, ...), condition=%wide.region_4.5_spmd.clone, body=%wide.region_3.4_spmd.clone.sunk | while | flops 181672768 | bytes 46007232 | solution.py:47
  182.5 2.9 convolution_add_fusion.12
  190.1 2.9 convolution_add_fusion.12
  197.6 2.9 convolution_add_fusion.12
  205.2 2.9 convolution_add_fusion.12
  212.8 2.9 convolution_add_fusion.12
  220.4 2.9 convolution_add_fusion.12
  227.9 2.9 convolution_add_fusion.12
  235.5 2.9 convolution_add_fusion.12
  238.4 2.4 convert_element_type.117
  240.8 2.4 convert_element_type.118
  245.7 105.5 %all-reduce.3.cloned.1.call-done = (f32[512,1024]{1,0:T(8,128)}, f32[1024,1024]{1,0:T(8,128)}, f32[1024,256]{1,0:T(8,128)}) async-done(((f32[512,1024]{1,0:T(8,128)}, f32[1024,1024]{1,0:T(8,128)}, f32[1024,256]{1,0:T(8,128)}), (f32[512,1024]{1,0:T(8,128)}, f32[1024,1024]{1,0:T(8,128)}, f32[1024,256]{1,0:T(8,128)})) %all-reduce.3.cloned.1.call-update) | async-done | bytes 7340048 | tf_op jit(solution)/shard_map/psum | solution.py:109
  351.2 2.4 broadcast_multiply_fusion.2
  356.6 2.5 broadcast_multiply_fusion
  359.0 30.3 %reduce-scatter.5.cloned.1.call-done = bf16[512,256]{1,0:T(8,128)(2,1)} async-done(((bf16[4096,256]{1,0:T(8,128)(2,1)}), bf16[512,256]{1,0:T(8,128)(2,1)}) %reduce-scatter.5.cloned.1.call-update) | async-done | bytes 262160 | tf_op jit(solution)/shard_map/reduce_scatter | solution.py:105
  (227 shorter events, 108.7 us)
Async XLA Ops:
  7.2 134.2 %copy-start = (bf16[1024,1024]{1,0:T(8,128)(2,1)S(1)}, bf16[1024,1024]{1,0:T(8,128)(2,1)}, u32[]{:S(2)}) copy-start(bf16[1024,1024]{1,0:T(8,128)(2,1)} %param.19) | copy-start | bytes 6291460
  7.2 34.3 %all-gather.3.cloned.1.call-start = ((), (), s32[]{:S(2)}) async-start(), calls=%async_computation.2 | async-start | bytes 2359296 | tf_op jit(solution)/shard_map/all_gather | solution.py:60
  7.9 130.6 %reduce-scatter.3.cloned.1.call-start = ((), (), s32[]{:S(2)}) async-start(), calls=%async_computation.3 | async-start | bytes 1310720 | tf_op jit(solution)/shard_map/reduce_scatter | solution.py:71
  13.1 32.6 %copy-start.18 = (s32[1,1,192]{2,1,0:T(1,128)S(1)}, s32[1,1,192]{2,1,0:T(1,128)}, u32[]{:S(2)}) copy-start(s32[1,1,192]{2,1,0:T(1,128)} %param.15) | copy-start | bytes 2308
  13.1 32.6 %copy-start.19 = (s32[1,1,192]{2,1,0:T(1,128)S(1)}, s32[1,1,192]{2,1,0:T(1,128)}, u32[]{:S(2)}) copy-start(s32[1,1,192]{2,1,0:T(1,128)} %param.16) | copy-start | bytes 2308
  49.3 1.7 copy-start.3
  57.1 1.7 copy-start.3
  64.9 1.7 copy-start.3
  72.8 1.7 copy-start.3
  111.2 64.9 %all-gather.5.cloned.1.call-start = ((), (), s32[]{:S(2)}) async-start(), calls=%async_computation.4 | async-start | bytes 1310720 | tf_op jit(solution)/shard_map/all_gather | solution.py:95
  141.4 3.5 copy-start.6
  141.4 2.6 copy-start.12
  141.4 2.6 copy-start.16
  145.0 1.7 copy-start.20
  145.0 1.7 copy-start.9
  146.7 3.0 copy-start.4
  149.4 201.8 %all-reduce.3.cloned.1.call-start = ((), (), s32[]{:S(2)}) async-start(), calls=%async_computation.6 | async-start | bytes 14680064 | tf_op jit(solution)/shard_map/psum | solution.py:109
  154.8 2.8 copy-start.11
  157.6 2.0 copy-start.7
  157.6 2.4 copy-start.21
  163.3 226.0 %reduce-scatter.5.cloned.1.call-start = ((), (), s32[]{:S(2)}) async-start(), calls=%async_computation.5 | async-start | bytes 2359296 | tf_op jit(solution)/shard_map/reduce_scatter | solution.py:105
  178.4 3.2 copy-start.2
  186.0 3.2 copy-start.2
  193.6 3.2 copy-start.2
  201.2 3.2 copy-start.2
  208.7 3.2 copy-start.2
  216.3 3.2 copy-start.2
  223.9 3.2 copy-start.2
  231.5 3.2 copy-start.2
  351.2 2.4 copy-start.8
  353.6 2.9 copy-start.5
  356.6 34.6 %copy-start.1 = (bf16[1024,1024]{1,0:T(8,128)(2,1)S(1)}, bf16[1024,1024]{1,0:T(8,128)(2,1)}, u32[]{:S(2)}) copy-start(bf16[1024,1024]{1,0:T(8,128)(2,1)} %param.19) | copy-start | bytes 6291460
  (9 other events, 12.6 us)
Sparse Core Ops, SparseCore 0:
  9.6 31.7 all-gather.2
  111.3 27.0 reduce-scatter.2
  149.5 26.6 all-gather.4
  183.7 167.4 all-reduce.2
  353.4 35.8 reduce-scatter.4
where the time goes:
time: 399 us; the launch traced here: 398 us
  waiting for transfers between devices  205 us (51%)
  matrix products  109 us (27%)
  local copies, waits for them, and re-layouts  45.6 us (11%)
  other arithmetic  22.9 us (6%)
  between operations  14 us (4%)
    psum x1, waiting for transfers between devices, shards(): lax.psum((local_in, local_mid, local_out), ('row', 'col'))  105 us
    dot_general x16, matrix products, one_group(): jnp.einsum('sn,sk->nk', add_table, lower, preferred_element_type=jnp.floa...  37.9 us
    reduce_scatter x1, waiting for transfers between devices, shards(): lax.psum_scatter(back.astype(jnp.bfloat16), 'row', scatter_dimension=0, t...  30.3 us
    all_gather x1, waiting for transfers between devices, shards(): column_feats = lax.all_gather(features, 'row', axis=0, tiled=True)  28.4 us
    reduce_scatter x1, waiting for transfers between devices, shards(): lax.psum_scatter(partial_value.astype(jnp.bfloat16), 'col', scatter_dimen...  27.2 us
    dot_general x16, matrix products, one_group(): jnp.einsum(form, part_blocks, picked, preferred_element_type=jnp.float32)  22.8 us
    dot_general x16, matrix products, one_group(): jnp.dot(pick_table, flat_source, preferred_element_type=jnp.float32)  19.7 us
    while x64, local copies, waits for them, and re-layouts  17.5 us
  transfers between devices with their start and end apart: 5, of which 5 were waited for; matrix products, arithmetic and copies ran while one was open for 23% of the time, Pallas kernels for 0%

commit v1 on v0

v1 whole, which is shorter than its diff:
```python
import functools
import math

import jax
import jax.numpy as jnp
from jax import lax
from jax.experimental import pallas as pl
from jax.experimental.pallas import tpu as pltpu
from jax.sharding import PartitionSpec as P

F32 = jnp.float32
BF16 = jnp.bfloat16
MESH = pl.DeviceIdType.MESH
VMEM_LIMIT = 50 * 1024 * 1024
UNROLL = 8


def in_vmem(count):
    return [pl.BlockSpec(memory_space=pltpu.VMEM)] * count


def nn(a, b):
    return lax.dot_general(a, b, (((1,), (0,)), ((), ())), preferred_element_type=F32)


def nt(a, b):
    return lax.dot_general(a, b, (((1,), (1,)), ((), ())), preferred_element_type=F32)


def tn(a, b):
    return lax.dot_general(a, b, (((0,), (0,)), ((), ())), preferred_element_type=F32)


def cell_kernel(transposed, from_ref, to_ref, count_ref, blocks_ref, src_ref, out_ref, acc):
    side = blocks_ref.shape[1]
    count = count_ref[0]
    acc[...] = jnp.zeros_like(acc)

    def body(step, carry):
        prods = []
        for u in range(UNROLL):
            s = step * UNROLL + u
            start = pl.multiple_of(from_ref[s] * side, side)
            rows = src_ref[pl.ds(start, side), :]
            block = jnp.where(s < count, blocks_ref[s], jnp.zeros((side, side), BF16))
            prods.append(tn(block, rows) if transposed else nn(block, rows))
        for u in range(UNROLL):
            s = step * UNROLL + u
            to = pl.multiple_of(to_ref[s] * side, side)
            acc[pl.ds(to, side), :] += prods[u]
        return carry

    lax.fori_loop(0, (count + UNROLL - 1) // UNROLL, body, 0)
    out_ref[...] = acc[...].astype(out_ref.dtype)


def cell_term(blocks, from_idx, to_idx, count, source, n_dst, transposed):
    slots, side, _ = blocks.shape
    feats = source.shape[1]
    smem = pl.BlockSpec(memory_space=pltpu.SMEM)
    return pl.pallas_call(
        functools.partial(cell_kernel, transposed),
        out_shape=jax.ShapeDtypeStruct((n_dst, feats), BF16),
        in_specs=[smem] * 3 + in_vmem(2),
        out_specs=in_vmem(1)[0],
        scratch_shapes=[pltpu.VMEM((n_dst, feats), F32)],
        compiler_params=pltpu.CompilerParams(vmem_limit_bytes=VMEM_LIMIT),
        cost_estimate=pl.CostEstimate(
            flops=2 * slots * side * side * feats,
            bytes_accessed=slots * side * side * 2 + 4 * n_dst * feats,
            transcendentals=0,
        ),
    )(from_idx, to_idx, count, blocks, source)


def middle_kernel(
    ncol, part, feat, cot, w_in, w_mid, w_out,
    upd, direct, rows_out, grads,
    land, joined, pre_one, back_two, act_one, act_two, gp_two, gp_one,
    send_a, recv_a, send_b, recv_b,
):
    r, c = lax.axis_index("row"), lax.axis_index("col")
    n, feats = feat.shape
    hid = w_mid.shape[0]
    half = n // 2

    barrier = pltpu.get_barrier_semaphore()
    for d in range(1, ncol):
        pl.semaphore_signal(barrier, inc=1, device_id=(r, lax.rem(c + d, ncol)), device_id_type=MESH)
    pl.semaphore_wait(barrier, ncol - 1)

    sums = []
    for d in range(1, ncol):
        peer = lax.rem(c + d, ncol)
        copy = pltpu.make_async_remote_copy(
            src_ref=part.at[pl.ds(pl.multiple_of(peer * n, n), n)],
            dst_ref=land.at[d - 1],
            send_sem=send_a.at[d - 1],
            recv_sem=recv_a.at[d - 1],
            device_id=(r, peer),
            device_id_type=MESH,
        )
        copy.start()
        sums.append(copy)

    joined[:, :feats] = feat[...]

    def early(i, carry):
        rows = pl.ds(pl.multiple_of(i * half, half), half)
        pre_one[rows, :] = nn(feat[rows, :], w_in[:feats, :])
        back_two[rows, :] = nt(cot[rows, :], w_out[...])
        return carry

    lax.fori_loop(0, 2, early, 0)

    for copy in sums:
        copy.wait()

    def network(i, carry):
        rows = pl.ds(pl.multiple_of(i * half, half), half)
        total = part[pl.ds(pl.multiple_of(c * n + i * half, half), half), :].astype(F32)
        for d in range(1, ncol):
            total = total + land[d - 1, rows, :].astype(F32)
        agg = total.astype(BF16)
        joined[rows, feats:] = agg
        one = pre_one[rows, :] + nn(agg, w_in[feats:, :])
        sig_one = jax.nn.sigmoid(one)
        a_one = (one * sig_one).astype(BF16)
        act_one[rows, :] = a_one
        pre_one[rows, :] = sig_one * (1.0 + one * (1.0 - sig_one))
        two = nn(a_one, w_mid[...])
        sig_two = jax.nn.sigmoid(two)
        act_two[rows, :] = (two * sig_two).astype(BF16)
        g_two = (back_two[rows, :] * (sig_two * (1.0 + two * (1.0 - sig_two)))).astype(BF16)
        gp_two[rows, :] = g_two
        g_one = (nt(g_two, w_mid[...]) * pre_one[rows, :]).astype(BF16)
        gp_one[rows, :] = g_one
        rows_out[pl.ds(pl.multiple_of(c * n + i * half, half), half), :] = nt(
            g_one, w_in[feats:, :]
        ).astype(BF16)
        return carry

    lax.fori_loop(0, 2, network, 0)

    gathers = []
    mine = rows_out.at[pl.ds(pl.multiple_of(c * n, n), n)]
    for d in range(1, ncol):
        copy = pltpu.make_async_remote_copy(
            src_ref=mine,
            dst_ref=mine,
            send_sem=send_b.at[d - 1],
            recv_sem=recv_b.at[d - 1],
            device_id=(r, lax.rem(c + d, ncol)),
            device_id_type=MESH,
        )
        copy.start()
        gathers.append(copy)

    def late(i, carry):
        rows = pl.ds(pl.multiple_of(i * half, half), half)
        direct[rows, :] = cot[rows, :].astype(F32) + nt(gp_one[rows, :], w_in[:feats, :])
        upd[rows, :] = (
            feat[rows, :].astype(F32) + nn(act_two[rows, :], w_out[...])
        ).astype(BF16)
        return carry

    lax.fori_loop(0, 2, late, 0)

    grads[:feats, :] = tn(cot[...], act_two[...]).astype(BF16)

    def mid_tile(i, carry):
        cols = pl.ds(pl.multiple_of(i * feats, feats), feats)
        grads[pl.ds(pl.multiple_of(feats + i * feats, feats), feats), :] = tn(
            act_one[:, cols], gp_two[...]
        ).astype(BF16)
        return carry

    lax.fori_loop(0, hid // feats, mid_tile, 0)

    def in_tile(i, carry):
        cols = pl.ds(pl.multiple_of(i * feats, feats), feats)
        grads[pl.ds(pl.multiple_of(feats + hid + i * feats, feats), feats), :] = tn(
            joined[:, cols], gp_one[...]
        ).astype(BF16)
        return carry

    lax.fori_loop(0, 2, in_tile, 0)

    for copy in gathers:
        copy.wait()


def middle(part, feat, cot, w_in, w_mid, w_out, ncol):
    n, feats = feat.shape
    hid = w_mid.shape[0]
    shape = jax.ShapeDtypeStruct
    return pl.pallas_call(
        functools.partial(middle_kernel, ncol),
        out_shape=(
            shape((n, feats), BF16),
            shape((n, feats), F32),
            shape((n * ncol, feats), BF16),
            shape((3 * feats + hid, hid), BF16),
        ),
        in_specs=in_vmem(6),
        out_specs=tuple(in_vmem(4)),
        scratch_shapes=[
            pltpu.VMEM((ncol - 1, n, feats), BF16),
            pltpu.VMEM((n, 2 * feats), BF16),
            pltpu.VMEM((n, hid), F32),
            pltpu.VMEM((n, hid), F32),
            pltpu.VMEM((n, hid), BF16),
            pltpu.VMEM((n, hid), BF16),
            pltpu.VMEM((n, hid), BF16),
            pltpu.VMEM((n, hid), BF16),
        ]
        + [pltpu.SemaphoreType.DMA((ncol - 1,))] * 4,
        compiler_params=pltpu.CompilerParams(
            collective_id=1, has_side_effects=True, vmem_limit_bytes=VMEM_LIMIT
        ),
        cost_estimate=pl.CostEstimate(
            flops=6 * n * (3 * feats + hid) * hid,
            bytes_accessed=4 * (3 * feats + hid) * hid,
            transcendentals=2 * n * hid,
        ),
    )(part, feat, cot, w_in, w_mid, w_out)


def tail_kernel(
    nrow, ncol, chunks, back, direct, grads,
    nodes, total,
    pair_land, pair_sum, chip_land, g_pair, g_half, g_col, g_colsum, g_chip,
    ps, pr, cs, cr, s0, r0, s1, r1, s2, r2, s3, r3, s4, r4, s5, r5,
):
    r, c = lax.axis_index("row"), lax.axis_index("col")
    chips = nrow // 2
    chip, core = r // 2, lax.rem(r, 2)
    other = 1 - core
    sibling = chip * 2 + other
    n = direct.shape[0]
    hid = grads.shape[1]
    width = hid // chips

    barrier = pltpu.get_barrier_semaphore()
    pl.semaphore_signal(barrier, inc=1, device_id=(sibling, c), device_id_type=MESH)
    for d in range(1, ncol):
        pl.semaphore_signal(barrier, inc=1, device_id=(r, lax.rem(c + d, ncol)), device_id_type=MESH)
    for d in range(1, chips):
        pl.semaphore_signal(
            barrier, inc=1, device_id=(lax.rem(chip + d, chips) * 2 + core, c), device_id_type=MESH
        )
    pl.semaphore_wait(barrier, ncol + chips - 1)

    def send(src, dst, ssem, rsem, device):
        copy = pltpu.make_async_remote_copy(
            src_ref=src, dst_ref=dst, send_sem=ssem, recv_sem=rsem,
            device_id=device, device_id_type=MESH,
        )
        copy.start()
        return copy

    def rows_at(start, size, unit):
        return pl.ds(pl.multiple_of(start, unit), size)

    pair = []
    for d in range(chips):
        z = lax.rem(chip + 1 + d, chips)
        pair.append(
            send(
                back.at[rows_at((z * 2 + other) * n, n, n)],
                pair_land.at[d], ps.at[d], pr.at[d], (sibling, c),
            )
        )

    offsets, halves = [], []
    at, at_half = 0, 0
    for rows in chunks:
        offsets.append(at)
        halves.append(at_half)
        at += rows
        at_half += rows // 2
    stage0 = []
    for q, rows in enumerate(chunks):
        h = rows // 2
        stage0.append(
            send(
                grads.at[rows_at(offsets[q] + other * h, h, 16)],
                g_pair.at[pl.ds(halves[q], h)], s0.at[q], r0.at[q], (sibling, c),
            )
        )

    across = []
    for d in range(chips):
        pair[d].wait()
        z = lax.rem(chip + 1 + d, chips)
        pair_sum[d] = (
            back[rows_at((z * 2 + core) * n, n, n), :].astype(F32) + pair_land[d].astype(F32)
        ).astype(BF16)
        if d < chips - 1:
            across.append(
                send(
                    pair_sum.at[d], chip_land.at[d], cs.at[d], cr.at[d], (z * 2 + core, c)
                )
            )

    stage1 = []
    for q, rows in enumerate(chunks):
        h = rows // 2
        m = h // ncol
        stage0[q].wait()
        g_half[pl.ds(halves[q], h), :] = (
            grads[rows_at(offsets[q] + core * h, h, 16), :].astype(F32)
            + g_pair[pl.ds(halves[q], h), :].astype(F32)
        ).astype(BF16)
        copies = []
        for d in range(1, ncol):
            peer = lax.rem(c + d, ncol)
            copies.append(
                send(
                    g_half.at[rows_at(halves[q] + peer * m, m, 16)],
                    g_col.at[d - 1, pl.ds(halves[q] // ncol, m)],
                    s1.at[q, d - 1], r1.at[q, d - 1], (r, peer),
                )
            )
        stage1.append(copies)

    stage2 = []
    for q, rows in enumerate(chunks):
        h = rows // 2
        m = h // ncol
        base = halves[q] // ncol
        for copy in stage1[q]:
            copy.wait()
        value = g_half[rows_at(halves[q] + c * m, m, 16), :].astype(F32)
        for d in range(1, ncol):
            value = value + g_col[d - 1, pl.ds(base, m), :].astype(F32)
        g_colsum[pl.ds(base, m), :] = value.astype(BF16)
        copies = []
        for d in range(1, chips):
            z = lax.rem(chip + d, chips)
            copies.append(
                send(
                    g_colsum.at[pl.ds(base, m), rows_at(z * width, width, width)],
                    g_chip.at[d - 1, pl.ds(base, m)],
                    s2.at[q, d - 1], r2.at[q, d - 1], (z * 2 + core, c),
                )
            )
        stage2.append(copies)

    stage3 = []
    for q, rows in enumerate(chunks):
        h = rows // 2
        m = h // ncol
        base = halves[q] // ncol
        for copy in stage2[q]:
            copy.wait()
        columns = rows_at(chip * width, width, width)
        value = g_colsum[pl.ds(base, m), columns].astype(F32)
        for d in range(1, chips):
            value = value + g_chip[d - 1, pl.ds(base, m), :].astype(F32)
        spot = total.at[rows_at(offsets[q] + core * h + c * m, m, 16), columns]
        spot[...] = value.astype(BF16)
        copies = []
        for d in range(1, chips):
            z = lax.rem(chip + d, chips)
            copies.append(send(spot, spot, s3.at[q, d - 1], r3.at[q, d - 1], (z * 2 + core, c)))
        stage3.append(copies)

    stage4 = []
    for q, rows in enumerate(chunks):
        h = rows // 2
        m = h // ncol
        for copy in stage3[q]:
            copy.wait()
        spot = total.at[rows_at(offsets[q] + core * h + c * m, m, 16)]
        copies = []
        for d in range(1, ncol):
            copies.append(
                send(spot, spot, s4.at[q, d - 1], r4.at[q, d - 1], (r, lax.rem(c + d, ncol)))
            )
        stage4.append(copies)

    for copy in across:
        copy.wait()
    value = direct[...] + pair_sum[chips - 1].astype(F32)
    for d in range(chips - 1):
        value = value + chip_land[d].astype(F32)
    nodes[...] = value.astype(BF16)

    stage5 = []
    for q, rows in enumerate(chunks):
        h = rows // 2
        for copy in stage4[q]:
            copy.wait()
        spot = total.at[rows_at(offsets[q] + core * h, h, 16)]
        stage5.append(send(spot, spot, s5.at[q], r5.at[q], (sibling, c)))
    for copy in stage5:
        copy.wait()


def tail(back, direct, grads, nrow, ncol):
    n, feats = direct.shape
    rows, hid = grads.shape
    chips = nrow // 2
    unit = 32 * ncol
    first = rows // 3 // unit * unit
    chunks = (first, first, rows - 2 * first)
    parts = len(chunks)
    shape = jax.ShapeDtypeStruct
    dma = pltpu.SemaphoreType.DMA
    return pl.pallas_call(
        functools.partial(tail_kernel, nrow, ncol, chunks),
        out_shape=(shape((n, feats), BF16), shape((rows, hid), BF16)),
        in_specs=in_vmem(3),
        out_specs=tuple(in_vmem(2)),
        scratch_shapes=[
            pltpu.VMEM((chips, n, feats), BF16),
            pltpu.VMEM((chips, n, feats), BF16),
            pltpu.VMEM((chips - 1, n, feats), BF16),
            pltpu.VMEM((rows // 2, hid), BF16),
            pltpu.VMEM((rows // 2, hid), BF16),
            pltpu.VMEM((ncol - 1, rows // 2 // ncol, hid), BF16),
            pltpu.VMEM((rows // 2 // ncol, hid), BF16),
            pltpu.VMEM((chips - 1, rows // 2 // ncol, hid // chips), BF16),
        ]
        + [dma((chips,))] * 2
        + [dma((chips - 1,))] * 2
        + [dma((parts,))] * 2
        + [dma((parts, ncol - 1))] * 2
        + [dma((parts, chips - 1))] * 4
        + [dma((parts, ncol - 1))] * 2
        + [dma((parts,))] * 2,
        compiler_params=pltpu.CompilerParams(
            collective_id=2, has_side_effects=True, vmem_limit_bytes=VMEM_LIMIT
        ),
    )(back, direct, grads)


def shards(features, blocks, block_rows, block_cols, block_count, w_in, w_mid, w_out, cotangent):
    nrow, ncol = lax.axis_size("row"), lax.axis_size("col")
    node_dev, feats = features.shape
    hid = w_mid.shape[0]
    cell_blocks = blocks[0, 0]
    rows_here = block_rows[0, 0]
    cols_here = block_cols[0, 0]
    count = block_count[0]
    column_feats = lax.all_gather(features, "row", axis=0, tiled=True)
    part = cell_term(
        cell_blocks, cols_here, rows_here, count, column_feats, node_dev * ncol, False
    )
    updated, direct, row_grads, grads = middle(
        part, features, cotangent, w_in, w_mid, w_out, ncol
    )
    back = cell_term(
        cell_blocks, rows_here, cols_here, count, row_grads, node_dev * nrow, True
    )
    grad_nodes, total = tail(back, direct, grads, nrow, ncol)
    ratio = 1.0 / math.sqrt(node_dev * nrow * ncol)
    total = total.astype(F32) * ratio
    return (
        updated,
        grad_nodes,
        total[feats + hid :],
        total[feats : feats + hid],
        total[:feats].T,
    )


def solution(mesh):
    placed = (
        P(("row", "col"), None),
        P("row", "col", None, None, None),
        P("row", "col", None),
        P("row", "col", None),
        P("row", "col"),
        P(),
        P(),
        P(),
        P(("row", "col"), None),
    )
    return jax.shard_map(
        shards,
        mesh=mesh,
        in_specs=placed,
        out_specs=(P(("row", "col"), None), P(("row", "col"), None), P(), P(), P()),
        check_vma=False,
    )
```

time: 399 us -> 178 us (0.45)
  waiting for transfers between devices: 205 us -> 28.4 us
  Pallas kernels: 0 us -> 117 us
  matrix products: 109 us -> 0 us
  local copies, waits for them, and re-layouts: 45.6 us -> 13.7 us
  other arithmetic: 22.9 us -> 3.07 us
    pallas_call x0 -> x4, Pallas kernels: none -> 117 us  [the longest x1 77.3 us: tail(): pl.pallas_call(functools.partial(tail_kernel, nrow, ncol, chunks), out_sh...]
    dot_general x73 -> x0, matrix products: 109 us -> none  [the longest x16 37.9 us: one_group(): jnp.einsum('sn,sk->nk', add_table, lower, preferred_element_type=jnp.floa...]
    psum x1 -> x0, waiting for transfers between devices: 105 us -> none  [shards(): lax.psum((local_in, local_mid, local_out), ('row', 'col'))]
    reduce_scatter x2 -> x0, waiting for transfers between devices: 57.5 us -> none  [the longest x1 30.3 us: shards(): lax.psum_scatter(back.astype(jnp.bfloat16), 'row', scatter_dimension=0, t...]
    while x64 -> x0, local copies, waits for them, and re-layouts: 17.5 us -> none
    all_gather x1 -> x0, waiting for transfers between devices: 12.8 us -> none  [shards(): row_grads = lax.all_gather(grad_agg, 'col', axis=0, tiled=True)]
    lt x16 -> x0, other arithmetic: 10.4 us -> none  [one_group(): live = start + jnp.arange(width, dtype=jnp.int32) < count]
    convert_element_type x3 -> x0, other arithmetic: 5.99 us -> none  [the longest x1 2.41 us: shards(): back.astype(jnp.bfloat16)]
  transfers between devices with their start and end apart: 5 -> 1, of which waited for: 5 -> 1; matrix products, arithmetic and copies ran while one was open for 23% -> 3% of each run, Pallas kernels for 0% -> 0%
where the time goes in v1:
time: 178 us; the launch traced here: 177 us
  Pallas kernels  117 us (66%)
  waiting for transfers between devices  28.4 us (16%)
  between operations  14.8 us (8%)
  local copies, waits for them, and re-layouts  13.7 us (8%)
  other arithmetic  3.07 us (2%)
    pallas_call x1, Pallas kernels, tail(): pl.pallas_call(functools.partial(tail_kernel, nrow, ncol, chunks), out_sh...  77.3 us
    pallas_call x1, Pallas kernels, middle(): pl.pallas_call(functools.partial(middle_kernel, ncol), out_shape=(shape((...  34.6 us
    all_gather x1, waiting for transfers between devices, shards(): column_feats = lax.all_gather(features, 'row', axis=0, tiled=True)  27.7 us
    unnamed x16, local copies, waits for them, and re-layouts  9.5 us
    pallas_call x2, Pallas kernels, cell_term(): pl.pallas_call(functools.partial(cell_kernel, transposed), out_shape=jax....  5.5 us
  transfers between devices with their start and end apart: 1, of which 1 were waited for; matrix products, arithmetic and copies ran while one was open for 3% of the time, Pallas kernels for 0%

profile of v1, /device:TPU:0, one launch (start us, length us, event | category | flops | bytes accessed | tf_op | source)
XLA Modules:
  0.0 177.4 jit_solution(7704375449744245144)
XLA Ops:
  7.2 0.0 copy-start.2
  7.2 0.0 copy-start.3
  7.2 0.0 all-gather.2.cloned.1.call-start
  7.2 0.7 all-gather.2.cloned.1.call-update
  8.6 0.0 copy-start.1
  8.6 0.0 copy-start.4
  8.6 0.0 copy-start.5
  8.6 5.2 %copy.14 = bf16[1,1,192,64,64]{4,3,2,1,0:T(8,128)(2,1)} copy(bf16[1,1,192,64,64]{2,4,3,1,0:T(8,128)(2,1)} %param.10) | data formatting | bytes 3145728 | tf_op args[1]
  13.8 27.7 %all-gather.2.cloned.1.call-done.src_ref = bf16[4096,256]{1,0:T(8,128)(2,1)} async-done(((bf16[512,256]{1,0:T(8,128)(2,1)}), bf16[4096,256]{1,0:T(8,128)(2,1)}) %all-gather.2.cloned.1.call-update) | async-done | bytes 2097168 | tf_op jit(solution)/shard_map/all_gather | solution.py:447
  41.5 0.0 copy-done.2
  41.5 0.0 copy-done.3
  41.5 0.0 copy-start
  41.5 1.6 copy-done
  43.1 2.6 %shard_map.128.part = bf16[2048,256]{1,0:T(8,128)(2,1)S(1)} custom-call(s32[192]{0:T(256)S(1)} %bitcast.8, s32[192]{0:T(256)S(1)} %bitcast.10, s32[1]{0:T(128)} %bitcast.6.count_ref, bf16[192,64,64]{2,1,0:T(8,128)(2,1)} %bitcast.12, bf16[4096,256]{1,0:T(8,128)(2,1)S(1)} %copy-done), custom_call_target="tpu_custom_call" | custom-call | flops 402653184 | bytes 3670016 | tf_op jit(solution)/shard_map/pallas_call | solution.py:61
  45.6 0.0 copy-done.1
  45.7 0.0 copy-done.4
  45.7 0.0 copy-done.5
  45.7 34.6 %shard_map.129 = (bf16[512,256]{1,0:T(8,128)(2,1)S(1)}, f32[512,256]{1,0:T(8,128)S(1)}, bf16[2048,256]{1,0:T(8,128)(2,1)S(1)}, bf16[1792,1024]{1,0:T(8,128)(2,1)}) custom-call(bf16[2048,256]{1,0:T(8,128)(2,1)S(1)} %shard_map.128.part, bf16[512,256]{1,0:T(8,128)(2,1)S(1)} %copy-done.1, bf16[512,256]{1,0:T(8,128)(2,1)S(1)} %copy-done.5, ...), custom_call_target="tpu_custom_call" | custom-call | flops 5637144576 | bytes 7340032 | tf_op jit(solution)/shard_map/pallas_call | solution.py:197
  80.3 2.9 %shard_map.130.back = bf16[4096,256]{1,0:T(8,128)(2,1)S(1)} custom-call(s32[192]{0:T(256)S(1)} %bitcast.11, s32[192]{0:T(256)S(1)} %bitcast.9, s32[1]{0:T(128)} %bitcast.7.count_ref, bf16[192,64,64]{2,1,0:T(8,128)(2,1)} %bitcast.13, bf16[2048,256]{1,0:T(8,128)(2,1)S(1)} %get-tuple-element.12.src_ref), custom_call_target="tpu_custom_call" | custom-call | flops 402653184 | bytes 5767168 | tf_op jit(solution)/shard_map/pallas_call | solution.py:61
  83.2 77.3 %shard_map.131 = (bf16[512,256]{1,0:T(8,128)(2,1)S(1)}, bf16[1792,1024]{1,0:T(8,128)(2,1)}) custom-call(bf16[4096,256]{1,0:T(8,128)(2,1)S(1)} %shard_map.130.back, f32[512,256]{1,0:T(8,128)S(1)} %get-tuple-element.13.direct, bf16[1792,1024]{1,0:T(8,128)(2,1)} %get-tuple-element.14.grads), custom_call_target="tpu_custom_call" | custom-call | tf_op jit(solution)/shard_map/pallas_call | solution.py:411
  160.5 3.1 %convert_multiply_fusion = f32[1792,1024]{1,0:T(8,128)S(1)} fusion(bf16[1792,1024]{1,0:T(8,128)(2,1)} %get-tuple-element.16), kind=kLoop, calls=%fused_computation | loop fusion | flops 3670016 | bytes 11010048 | tf_op jit(solution)/shard_map/mul | solution.py:459
  163.6 0.1 slice_bitcast_fusion
  163.7 1.6 slice.12
  165.3 2.5 %slice.13 = f32[1024,1024]{1,0:T(8,128)} slice(f32[1792,1024]{1,0:T(8,128)S(1)} %convert_multiply_fusion), slice={[256:1280], [0:1024]} | slice | bytes 8388608 | tf_op jit(solution)/shard_map/slice | solution.py:464
  167.8 1.3 copy.15
  169.1 0.7 copy.19
  169.8 0.7 copy.20
Async XLA Ops:
  7.2 34.3 %copy-start.2 = (s32[1,1,192]{2,1,0:T(1,128)S(1)}, s32[1,1,192]{2,1,0:T(1,128)}, u32[]{:S(2)}) copy-start(s32[1,1,192]{2,1,0:T(1,128)} %param.12) | copy-start | bytes 2308
  7.2 34.3 %copy-start.3 = (s32[1,1,192]{2,1,0:T(1,128)S(1)}, s32[1,1,192]{2,1,0:T(1,128)}, u32[]{:S(2)}) copy-start(s32[1,1,192]{2,1,0:T(1,128)} %param.11) | copy-start | bytes 2308
  7.2 34.3 %all-gather.2.cloned.1.call-start = ((), (), s32[]{:S(2)}) async-start(), calls=%async_computation | async-start | bytes 2359296 | tf_op jit(solution)/shard_map/all_gather | solution.py:447
  8.6 37.1 %copy-start.1 = (bf16[512,256]{1,0:T(8,128)(2,1)S(1)}, bf16[512,256]{1,0:T(8,128)(2,1)}, u32[]{:S(2)}) copy-start(bf16[512,256]{1,0:T(8,128)(2,1)} %feat.1) | copy-start | bytes 786436
  8.6 37.1 %copy-start.4 = (bf16[1024,256]{1,0:T(8,128)(2,1)S(1)}, bf16[1024,256]{1,0:T(8,128)(2,1)}, u32[]{:S(2)}) copy-start(bf16[1024,256]{1,0:T(8,128)(2,1)} %w_out.1) | copy-start | bytes 1572868
  8.6 37.1 %copy-start.5 = (bf16[512,256]{1,0:T(8,128)(2,1)S(1)}, bf16[512,256]{1,0:T(8,128)(2,1)}, u32[]{:S(2)}) copy-start(bf16[512,256]{1,0:T(8,128)(2,1)} %cot.1) | copy-start | bytes 786436
  41.5 1.6 copy-start
Sparse Core Ops, SparseCore 0:
  9.6 31.7 all-gather.1

commit v2 on v1

--- a/solution.py
+++ b/solution.py
@@ -73,35 +73,51 @@
     )(from_idx, to_idx, count, blocks, source)
 
 
+def chunk_list(feats, hid):
+    mid = hid // 2
+    return (
+        (0, feats),
+        (feats, mid),
+        (feats + mid, mid),
+        (feats + hid, feats),
+        (2 * feats + hid, feats),
+    )
+
+
 def middle_kernel(
     ncol, part, feat, cot, w_in, w_mid, w_out,
-    upd, direct, rows_out, grads,
-    land, joined, pre_one, back_two, act_one, act_two, gp_two, gp_one,
-    send_a, recv_a, send_b, recv_b,
+    upd, direct, rows_out, g_half,
+    grads, g_pair, land, joined, pre_one, back_two, act_one, act_two, gp_two, gp_one,
+    send_a, recv_a, send_b, recv_b, send_c, recv_c,
 ):
     r, c = lax.axis_index("row"), lax.axis_index("col")
     n, feats = feat.shape
     hid = w_mid.shape[0]
     half = n // 2
+    core = lax.rem(r, 2)
+    sibling = r + 1 - 2 * core
 
     barrier = pltpu.get_barrier_semaphore()
+    pl.semaphore_signal(barrier, inc=1, device_id=(sibling, c), device_id_type=MESH)
     for d in range(1, ncol):
         pl.semaphore_signal(barrier, inc=1, device_id=(r, lax.rem(c + d, ncol)), device_id_type=MESH)
-    pl.semaphore_wait(barrier, ncol - 1)
+    pl.semaphore_wait(barrier, ncol)
 
     sums = []
-    for d in range(1, ncol):
-        peer = lax.rem(c + d, ncol)
-        copy = pltpu.make_async_remote_copy(
-            src_ref=part.at[pl.ds(pl.multiple_of(peer * n, n), n)],
-            dst_ref=land.at[d - 1],
-            send_sem=send_a.at[d - 1],
-            recv_sem=recv_a.at[d - 1],
-            device_id=(r, peer),
-            device_id_type=MESH,
-        )
-        copy.start()
-        sums.append(copy)
+    for i in range(2):
+        sums.append([])
+        for d in range(1, ncol):
+            peer = lax.rem(c + d, ncol)
+            copy = pltpu.make_async_remote_copy(
+                src_ref=part.at[pl.ds(pl.multiple_of(peer * n + i * half, half), half)],
+                dst_ref=land.at[d - 1, pl.ds(i * half, half)],
+                send_sem=send_a.at[i, d - 1],
+                recv_sem=recv_a.at[i, d - 1],
+                device_id=(r, peer),
+                device_id_type=MESH,
+            )
+            copy.start()
+            sums[i].append(copy)
 
     joined[:, :feats] = feat[...]
 
@@ -113,11 +129,11 @@
 
     lax.fori_loop(0, 2, early, 0)
 
-    for copy in sums:
-        copy.wait()
-
-    def network(i, carry):
-        rows = pl.ds(pl.multiple_of(i * half, half), half)
+    gathers = []
+    for i in range(2):
+        for copy in sums[i]:
+            copy.wait()
+        rows = pl.ds(i * half, half)
         total = part[pl.ds(pl.multiple_of(c * n + i * half, half), half), :].astype(F32)
         for d in range(1, ncol):
             total = total + land[d - 1, rows, :].astype(F32)
@@ -138,23 +154,59 @@
         rows_out[pl.ds(pl.multiple_of(c * n + i * half, half), half), :] = nt(
             g_one, w_in[feats:, :]
         ).astype(BF16)
-        return carry
-
-    lax.fori_loop(0, 2, network, 0)
-
-    gathers = []
-    mine = rows_out.at[pl.ds(pl.multiple_of(c * n, n), n)]
-    for d in range(1, ncol):
+        mine = rows_out.at[pl.ds(pl.multiple_of(c * n + i * half, half), half)]
+        for d in range(1, ncol):
+            copy = pltpu.make_async_remote_copy(
+                src_ref=mine,
+                dst_ref=mine,
+                send_sem=send_b.at[i, d - 1],
+                recv_sem=recv_b.at[i, d - 1],
+                device_id=(r, lax.rem(c + d, ncol)),
+                device_id_type=MESH,
+            )
+            copy.start()
+            gathers.append(copy)
+
+    pairs = []
+
+    def trade(q):
+        at, rows = chunk_list(feats, hid)[q]
+        h = rows // 2
         copy = pltpu.make_async_remote_copy(
-            src_ref=mine,
-            dst_ref=mine,
-            send_sem=send_b.at[d - 1],
-            recv_sem=recv_b.at[d - 1],
-            device_id=(r, lax.rem(c + d, ncol)),
+            src_ref=grads.at[pl.ds(pl.multiple_of(at + (1 - core) * h, h), h)],
+            dst_ref=g_pair.at[pl.ds(at // 2, h)],
+            send_sem=send_c.at[q],
+            recv_sem=recv_c.at[q],
+            device_id=(sibling, c),
             device_id_type=MESH,
         )
         copy.start()
-        gathers.append(copy)
+        pairs.append(copy)
+
+    grads[:feats, :] = tn(cot[...], act_two[...]).astype(BF16)
+    trade(0)
+
+    def mid_tile(i, carry):
+        cols = pl.ds(pl.multiple_of(i * feats, feats), feats)
+        grads[pl.ds(pl.multiple_of(feats + i * feats, feats), feats), :] = tn(
+            act_one[:, cols], gp_two[...]
+        ).astype(BF16)
+        return carry
+
+    lax.fori_loop(0, hid // feats, mid_tile, 0)
+    trade(1)
+    trade(2)
+
+    def in_tile(i, carry):
+        cols = pl.ds(pl.multiple_of(i * feats, feats), feats)
+        grads[pl.ds(pl.multiple_of(feats + hid + i * feats, feats), feats), :] = tn(
+            joined[:, cols], gp_one[...]
+        ).astype(BF16)
+        return carry
+
+    lax.fori_loop(0, 2, in_tile, 0)
+    trade(3)
+    trade(4)
 
     def late(i, carry):
         rows = pl.ds(pl.multiple_of(i * half, half), half)
@@ -166,25 +218,13 @@
 
     lax.fori_loop(0, 2, late, 0)
 
-    grads[:feats, :] = tn(cot[...], act_two[...]).astype(BF16)
-
-    def mid_tile(i, carry):
-        cols = pl.ds(pl.multiple_of(i * feats, feats), feats)
-        grads[pl.ds(pl.multiple_of(feats + i * feats, feats), feats), :] = tn(
-            act_one[:, cols], gp_two[...]
+    for q, (at, rows) in enumerate(chunk_list(feats, hid)):
+        h = rows // 2
+        pairs[q].wait()
+        g_half[pl.ds(at // 2, h), :] = (
+            grads[pl.ds(pl.multiple_of(at + core * h, h), h), :].astype(F32)
+            + g_pair[pl.ds(at // 2, h), :].astype(F32)
         ).astype(BF16)
-        return carry
-
-    lax.fori_loop(0, hid // feats, mid_tile, 0)
-
-    def in_tile(i, carry):
-        cols = pl.ds(pl.multiple_of(i * feats, feats), feats)
-        grads[pl.ds(pl.multiple_of(feats + hid + i * feats, feats), feats), :] = tn(
-            joined[:, cols], gp_one[...]
-        ).astype(BF16)
-        return carry
-
-    lax.fori_loop(0, 2, in_tile, 0)
 
     for copy in gathers:
         copy.wait()
@@ -200,11 +240,13 @@
             shape((n, feats), BF16),
             shape((n, feats), F32),
             shape((n * ncol, feats), BF16),
-            shape((3 * feats + hid, hid), BF16),
+            shape(((3 * feats + hid) // 2, hid), BF16),
         ),
         in_specs=in_vmem(6),
         out_specs=tuple(in_vmem(4)),
         scratch_shapes=[
+            pltpu.VMEM((3 * feats + hid, hid), BF16),
+            pltpu.VMEM(((3 * feats + hid) // 2, hid), BF16),
             pltpu.VMEM((ncol - 1, n, feats), BF16),
             pltpu.VMEM((n, 2 * feats), BF16),
             pltpu.VMEM((n, hid), F32),
@@ -214,7 +256,8 @@
             pltpu.VMEM((n, hid), BF16),
             pltpu.VMEM((n, hid), BF16),
         ]
-        + [pltpu.SemaphoreType.DMA((ncol - 1,))] * 4,
+        + [pltpu.SemaphoreType.DMA((2, ncol - 1))] * 4
+        + [pltpu.SemaphoreType.DMA((5,))] * 2,
         compiler_params=pltpu.CompilerParams(
             collective_id=1, has_side_effects=True, vmem_limit_bytes=VMEM_LIMIT
         ),
@@ -227,19 +270,23 @@
 
 
 def tail_kernel(
-    nrow, ncol, chunks, back, direct, grads,
-    nodes, total,
-    pair_land, pair_sum, chip_land, g_pair, g_half, g_col, g_colsum, g_chip,
-    ps, pr, cs, cr, s0, r0, s1, r1, s2, r2, s3, r3, s4, r4, s5, r5,
+    nrow, ncol, back, direct, g_half,
+    nodes, t_out, t_mid, t_in,
+    pair_land, pair_sum, chip_land, g_col, g_colsum, g_chip, g_first,
+    ps, pr, cs, cr, s1, r1, s2, r2, s3, r3, s4, r4, s5, r5,
 ):
     r, c = lax.axis_index("row"), lax.axis_index("col")
     chips = nrow // 2
     chip, core = r // 2, lax.rem(r, 2)
     other = 1 - core
     sibling = chip * 2 + other
-    n = direct.shape[0]
-    hid = grads.shape[1]
+    n, feats = direct.shape
+    hid = g_half.shape[1]
     width = hid // chips
+    chunks = chunk_list(feats, hid)
+    homes = (
+        (g_first, 0), (t_mid, 0), (t_mid, hid // 2), (t_in, 0), (t_in, feats)
+    )
 
     barrier = pltpu.get_barrier_semaphore()
     pl.semaphore_signal(barrier, inc=1, device_id=(sibling, c), device_id_type=MESH)
@@ -272,66 +319,48 @@
             )
         )
 
-    offsets, halves = [], []
-    at, at_half = 0, 0
-    for rows in chunks:
-        offsets.append(at)
-        halves.append(at_half)
-        at += rows
-        at_half += rows // 2
-    stage0 = []
-    for q, rows in enumerate(chunks):
-        h = rows // 2
-        stage0.append(
-            send(
-                grads.at[rows_at(offsets[q] + other * h, h, 16)],
-                g_pair.at[pl.ds(halves[q], h)], s0.at[q], r0.at[q], (sibling, c),
+    stage1 = []
+    for q, (at, rows) in enumerate(chunks):
+        m = rows // 2 // ncol
+        copies = []
+        for d in range(1, ncol):
+            peer = lax.rem(c + d, ncol)
+            copies.append(
+                send(
+                    g_half.at[rows_at(at // 2 + peer * m, m, 16)],
+                    g_col.at[d - 1, pl.ds(at // 2 // ncol, m)],
+                    s1.at[q, d - 1], r1.at[q, d - 1], (r, peer),
+                )
             )
+        stage1.append(copies)
+
+    across = []
+
+    def across_send(d):
+        z = lax.rem(chip + 1 + d, chips)
+        across.append(
+            send(pair_sum.at[d], chip_land.at[d], cs.at[d], cr.at[d], (z * 2 + core, c))
         )
 
-    across = []
+    late = chips // 4
     for d in range(chips):
         pair[d].wait()
         z = lax.rem(chip + 1 + d, chips)
         pair_sum[d] = (
             back[rows_at((z * 2 + core) * n, n, n), :].astype(F32) + pair_land[d].astype(F32)
         ).astype(BF16)
-        if d < chips - 1:
-            across.append(
-                send(
-                    pair_sum.at[d], chip_land.at[d], cs.at[d], cr.at[d], (z * 2 + core, c)
-                )
-            )
-
-    stage1 = []
-    for q, rows in enumerate(chunks):
-        h = rows // 2
-        m = h // ncol
-        stage0[q].wait()
-        g_half[pl.ds(halves[q], h), :] = (
-            grads[rows_at(offsets[q] + core * h, h, 16), :].astype(F32)
-            + g_pair[pl.ds(halves[q], h), :].astype(F32)
-        ).astype(BF16)
-        copies = []
-        for d in range(1, ncol):
-            peer = lax.rem(c + d, ncol)
-            copies.append(
-                send(
-                    g_half.at[rows_at(halves[q] + peer * m, m, 16)],
-                    g_col.at[d - 1, pl.ds(halves[q] // ncol, m)],
-                    s1.at[q, d - 1], r1.at[q, d - 1], (r, peer),
-                )
-            )
-        stage1.append(copies)
-
-    stage2 = []
-    for q, rows in enumerate(chunks):
-        h = rows // 2
-        m = h // ncol
-        base = halves[q] // ncol
+        if d < chips - 1 - late:
+            across_send(d)
+
+    stage2, stage3, stage4, stage5 = [], [], [], []
+
+    def over_chips(q):
+        at, rows = chunks[q]
+        m = rows // 2 // ncol
+        base = at // 2 // ncol
         for copy in stage1[q]:
             copy.wait()
-        value = g_half[rows_at(halves[q] + c * m, m, 16), :].astype(F32)
+        value = g_half[rows_at(at // 2 + c * m, m, 16), :].astype(F32)
         for d in range(1, ncol):
             value = value + g_col[d - 1, pl.ds(base, m), :].astype(F32)
         g_colsum[pl.ds(base, m), :] = value.astype(BF16)
@@ -347,18 +376,19 @@
             )
         stage2.append(copies)
 
-    stage3 = []
-    for q, rows in enumerate(chunks):
+    def back_over_chips(q):
+        at, rows = chunks[q]
+        home, first = homes[q]
         h = rows // 2
         m = h // ncol
-        base = halves[q] // ncol
+        base = at // 2 // ncol
         for copy in stage2[q]:
             copy.wait()
         columns = rows_at(chip * width, width, width)
         value = g_colsum[pl.ds(base, m), columns].astype(F32)
         for d in range(1, chips):
             value = value + g_chip[d - 1, pl.ds(base, m), :].astype(F32)
-        spot = total.at[rows_at(offsets[q] + core * h + c * m, m, 16), columns]
+        spot = home.at[rows_at(first + core * h + c * m, m, 16), columns]
         spot[...] = value.astype(BF16)
         copies = []
         for d in range(1, chips):
@@ -366,13 +396,14 @@
             copies.append(send(spot, spot, s3.at[q, d - 1], r3.at[q, d - 1], (z * 2 + core, c)))
         stage3.append(copies)
 
-    stage4 = []
-    for q, rows in enumerate(chunks):
+    def back_over_col(q):
+        _, rows = chunks[q]
+        home, first = homes[q]
         h = rows // 2
         m = h // ncol
         for copy in stage3[q]:
             copy.wait()
-        spot = total.at[rows_at(offsets[q] + core * h + c * m, m, 16)]
+        spot = home.at[rows_at(first + core * h + c * m, m, 16)]
         copies = []
         for d in range(1, ncol):
             copies.append(
@@ -380,52 +411,68 @@
             )
         stage4.append(copies)
 
+    def back_to_pair(q):
+        _, rows = chunks[q]
+        home, first = homes[q]
+        h = rows // 2
+        for copy in stage4[q]:
+            copy.wait()
+        spot = home.at[rows_at(first + core * h, h, 16)]
+        stage5.append(send(spot, spot, s5.at[q], r5.at[q], (sibling, c)))
+
+    parts = len(chunks)
+    for step in range(parts + 2):
+        if step < parts:
+            over_chips(step)
+        if 1 <= step <= parts:
+            back_over_chips(step - 1)
+        if step >= 2:
+            back_over_col(step - 2)
+    for d in range(chips - 1 - late, chips - 1):
+        across_send(d)
+    for q in range(parts - 1):
+        back_to_pair(q)
+    stage5[0].wait()
+    t_out[...] = jnp.transpose(g_first[...].astype(F32)).astype(BF16)
     for copy in across:
         copy.wait()
     value = direct[...] + pair_sum[chips - 1].astype(F32)
     for d in range(chips - 1):
         value = value + chip_land[d].astype(F32)
     nodes[...] = value.astype(BF16)
-
-    stage5 = []
-    for q, rows in enumerate(chunks):
-        h = rows // 2
-        for copy in stage4[q]:
-            copy.wait()
-        spot = total.at[rows_at(offsets[q] + core * h, h, 16)]
-        stage5.append(send(spot, spot, s5.at[q], r5.at[q], (sibling, c)))
-    for copy in stage5:
+    back_to_pair(parts - 1)
+    for copy in stage5[1:]:
         copy.wait()
 
 
-def tail(back, direct, grads, nrow, ncol):
+def tail(back, direct, g_half, nrow, ncol):
     n, feats = direct.shape
-    rows, hid = grads.shape
+    rows, hid = g_half.shape
     chips = nrow // 2
-    unit = 32 * ncol
-    first = rows // 3 // unit * unit
-    chunks = (first, first, rows - 2 * first)
-    parts = len(chunks)
+    parts = len(chunk_list(feats, hid))
     shape = jax.ShapeDtypeStruct
     dma = pltpu.SemaphoreType.DMA
     return pl.pallas_call(
-        functools.partial(tail_kernel, nrow, ncol, chunks),
-        out_shape=(shape((n, feats), BF16), shape((rows, hid), BF16)),
+        functools.partial(tail_kernel, nrow, ncol),
+        out_shape=(
+            shape((n, feats), BF16),
+            shape((hid, feats), BF16),
+            shape((hid, hid), BF16),
+            shape((2 * feats, hid), BF16),
+        ),
         in_specs=in_vmem(3),
-        out_specs=tuple(in_vmem(2)),
+        out_specs=tuple(in_vmem(4)),
         scratch_shapes=[
             pltpu.VMEM((chips, n, feats), BF16),
             pltpu.VMEM((chips, n, feats), BF16),
             pltpu.VMEM((chips - 1, n, feats), BF16),
-            pltpu.VMEM((rows // 2, hid), BF16),
-            pltpu.VMEM((rows // 2, hid), BF16),
-            pltpu.VMEM((ncol - 1, rows // 2 // ncol, hid), BF16),
-            pltpu.VMEM((rows // 2 // ncol, hid), BF16),
-            pltpu.VMEM((chips - 1, rows // 2 // ncol, hid // chips), BF16),
+            pltpu.VMEM((ncol - 1, rows // ncol, hid), BF16),
+            pltpu.VMEM((rows // ncol, hid), BF16),
+            pltpu.VMEM((chips - 1, rows // ncol, hid // chips), BF16),
+            pltpu.VMEM((feats, hid), BF16),
         ]
         + [dma((chips,))] * 2
         + [dma((chips - 1,))] * 2
-        + [dma((parts,))] * 2
         + [dma((parts, ncol - 1))] * 2
         + [dma((parts, chips - 1))] * 4
         + [dma((parts, ncol - 1))] * 2
@@ -433,7 +480,116 @@
         compiler_params=pltpu.CompilerParams(
             collective_id=2, has_side_effects=True, vmem_limit_bytes=VMEM_LIMIT
         ),
-    )(back, direct, grads)
+    )(back, direct, g_half)
+
+
+def gather_kernel(nrow, feat, out, own_sem, ss, sr, rs, rr, ls, lr, fs, fr):
+    r, c = lax.axis_index("row"), lax.axis_index("col")
+    chips = nrow // 2
+    chip, core = r // 2, lax.rem(r, 2)
+    sibling = chip * 2 + 1 - core
+    n = feat.shape[0]
+    up, down = chip < chips - 1, chip > 0
+    above = lax.rem(chip + 1, chips) * 2 + core
+    below = lax.rem(chip + chips - 1, chips) * 2 + core
+
+    def spot(device):
+        return out.at[pl.ds(pl.multiple_of(device * n, n), n)]
+
+    def remote(src, dst, ssem, rsem, device):
+        return pltpu.make_async_remote_copy(
+            src_ref=src, dst_ref=dst, send_sem=ssem, recv_sem=rsem,
+            device_id=(device, c), device_id_type=MESH,
+        )
+
+    own = pltpu.make_async_copy(feat, spot(r), own_sem)
+    own.start()
+    barrier = pltpu.get_barrier_semaphore()
+    pl.semaphore_signal(barrier, inc=1, device_id=(sibling, c), device_id_type=MESH)
+
+    @pl.when(up)
+    def _():
+        pl.semaphore_signal(barrier, inc=1, device_id=(above, c), device_id_type=MESH)
+
+    @pl.when(down)
+    def _():
+        pl.semaphore_signal(barrier, inc=1, device_id=(below, c), device_id_type=MESH)
+
+    pl.semaphore_wait(barrier, 1 + up.astype(jnp.int32) + down.astype(jnp.int32))
+
+    @pl.when(up)
+    def _():
+        remote(feat, spot(r), rs.at[0], rr.at[0], above).start()
+
+    @pl.when(down)
+    def _():
+        remote(feat, spot(r), ls.at[0], lr.at[0], below).start()
+
+    near = remote(feat, spot(r), ss, sr, sibling)
+    near.start()
+
+    for k in range(1, chips):
+        @pl.when(chip >= k)
+        def _():
+            source = spot(lax.rem(chip - k + chips, chips) * 2 + core)
+            remote(source, source, rs.at[k - 1], rr.at[k - 1], below).wait_recv()
+
+            @pl.when(up)
+            def _():
+                remote(source, source, rs.at[k], rr.at[k], above).start()
+
+            remote(source, source, fs.at[0, k - 1], fr.at[0, k - 1], sibling).start()
+
+        @pl.when(chip + k < chips)
+        def _():
+            source = spot(lax.rem(chip + k, chips) * 2 + core)
+            remote(source, source, ls.at[k - 1], lr.at[k - 1], above).wait_recv()
+
+            @pl.when(down)
+            def _():
+                remote(source, source, ls.at[k], lr.at[k], below).start()
+
+            remote(source, source, fs.at[1, k - 1], fr.at[1, k - 1], sibling).start()
+
+    own.wait()
+    near.wait()
+    for k in range(chips):
+        @pl.when(up & (chip >= k))
+        def _():
+            remote(feat, spot(r), rs.at[k], rr.at[k], above).wait_send()
+
+        @pl.when(down & (chip + k < chips))
+        def _():
+            remote(feat, spot(r), ls.at[k], lr.at[k], below).wait_send()
+
+        if k:
+            @pl.when(chip >= k)
+            def _():
+                source = spot(lax.rem(chip - k + chips, chips) * 2 + core)
+                landed = spot(lax.rem(chip - k + chips, chips) * 2 + 1 - core)
+                remote(source, landed, fs.at[0, k - 1], fr.at[0, k - 1], sibling).wait()
+
+            @pl.when(chip + k < chips)
+            def _():
+                source = spot(lax.rem(chip + k, chips) * 2 + core)
+                landed = spot(lax.rem(chip + k, chips) * 2 + 1 - core)
+                remote(source, landed, fs.at[1, k - 1], fr.at[1, k - 1], sibling).wait()
+
+
+def gather(feat, nrow):
+    n, feats = feat.shape
+    chips = nrow // 2
+    dma = pltpu.SemaphoreType.DMA
+    return pl.pallas_call(
+        functools.partial(gather_kernel, nrow),
+        out_shape=jax.ShapeDtypeStruct((n * nrow, feats), BF16),
+        in_specs=in_vmem(1),
+        out_specs=in_vmem(1)[0],
+        scratch_shapes=[dma] * 3 + [dma((chips,))] * 4 + [dma((2, chips - 1))] * 2,
+        compiler_params=pltpu.CompilerParams(
+            collective_id=3, has_side_effects=True, vmem_limit_bytes=VMEM_LIMIT
+        ),
+    )(feat)
 
 
 def shards(features, blocks, block_rows, block_cols, block_count, w_in, w_mid, w_out, cotangent):
@@ -444,7 +600,7 @@
     rows_here = block_rows[0, 0]
     cols_here = block_cols[0, 0]
     count = block_count[0]
-    column_feats = lax.all_gather(features, "row", axis=0, tiled=True)
+    column_feats = gather(features, nrow)
     part = cell_term(
         cell_blocks, cols_here, rows_here, count, column_feats, node_dev * ncol, False
     )
@@ -454,15 +610,14 @@
     back = cell_term(
         cell_blocks, rows_here, cols_here, count, row_grads, node_dev * nrow, True
     )
-    grad_nodes, total = tail(back, direct, grads, nrow, ncol)
+    grad_nodes, sum_out, sum_mid, sum_in = tail(back, direct, grads, nrow, ncol)
     ratio = 1.0 / math.sqrt(node_dev * nrow * ncol)
-    total = total.astype(F32) * ratio
     return (
         updated,
         grad_nodes,
-        total[feats + hid :],
-        total[feats : feats + hid],
-        total[:feats].T,
+        sum_in.astype(F32) * ratio,
+        sum_mid.astype(F32) * ratio,
+        sum_out.astype(F32) * ratio,
     )
 
 

time: 178 us -> 143 us (0.80)
  waiting for transfers between devices: 28.4 us -> 0 us
  between operations: 14.8 us -> 1.43 us
  Pallas kernels: 117 us -> 126 us
  local copies, waits for them, and re-layouts: 13.7 us -> 7.88 us
  other arithmetic: 3.07 us -> 6.84 us
    all_gather x1 -> x0, waiting for transfers between devices: 27.7 us -> none  [shards(): column_feats = lax.all_gather(features, 'row', axis=0, tiled=True)]
    pallas_call x2, Pallas kernels: 5.5 us -> 12.1 us  [cell_term(): pl.pallas_call(functools.partial(cell_kernel, transposed), out_shape=jax....]
    pallas_call x1 -> x2, Pallas kernels: 77.3 us -> 83.8 us  [the longest x1 57.8 us: tail(): pl.pallas_call(functools.partial(tail_kernel, nrow, ncol), out_shape=(sha...]
    pallas_call x1, Pallas kernels: 34.6 us -> 30.4 us  [middle(): pl.pallas_call(functools.partial(middle_kernel, ncol), out_shape=(shape((...]
    slice x2 -> x0, local copies, waits for them, and re-layouts: 4.11 us -> none  [the longest x1 2.54 us: shards(): total[feats:feats + hid]]
    mul x1 -> x3, other arithmetic: 3.07 us -> 6.84 us  [the longest x1 4.2 us: shards(): sum_mid.astype(F32) * ratio]
    unnamed x16 -> x15, local copies, waits for them, and re-layouts: 9.5 us -> 7.88 us
  transfers between devices with their start and end apart: 1 -> 0, of which waited for: 1 -> 0; matrix products, arithmetic and copies ran while one was open for 3% -> 0% of each run, Pallas kernels for 0% -> 0%
where the time goes in v2:
time: 143 us; the launch traced here: 142 us
  Pallas kernels  126 us (88%)
  local copies, waits for them, and re-layouts  7.88 us (6%)
  other arithmetic  6.84 us (5%)
  between operations  1.43 us (1%)
    pallas_call x1, Pallas kernels, tail(): pl.pallas_call(functools.partial(tail_kernel, nrow, ncol), out_shape=(sha...  57.8 us
    pallas_call x1, Pallas kernels, middle(): pl.pallas_call(functools.partial(middle_kernel, ncol), out_shape=(shape((...  30.4 us
    pallas_call x1, Pallas kernels, gather(): pl.pallas_call(functools.partial(gather_kernel, nrow), out_shape=jax.Shap...  26 us
    pallas_call x2, Pallas kernels, cell_term(): pl.pallas_call(functools.partial(cell_kernel, transposed), out_shape=jax....  12.1 us
    unnamed x15, local copies, waits for them, and re-layouts  7.88 us
    mul x1, other arithmetic, shards(): sum_mid.astype(F32) * ratio  4.2 us

profile of v2, /device:TPU:0, one launch (start us, length us, event | category | flops | bytes accessed | tf_op | source)
XLA Modules:
  0.0 142.4 jit_solution(17362839500459184355)
XLA Ops:
  0.6 0.0 copy-start.1
  0.6 5.1 %copy.14 = bf16[1,1,192,64,64]{4,3,2,1,0:T(8,128)(2,1)} copy(bf16[1,1,192,64,64]{2,4,3,1,0:T(8,128)(2,1)} %param.10) | data formatting | bytes 3145728 | tf_op args[1]
  5.8 0.0 copy-start.2
  5.8 0.0 copy-start.3
  6.5 0.0 copy-done.1
  6.5 26.0 %shard_map.128.src_ref = bf16[4096,256]{1,0:T(8,128)(2,1)S(1)} custom-call(bf16[512,256]{1,0:T(8,128)(2,1)S(1)} %copy-done.1), custom_call_target="tpu_custom_call" | custom-call | tf_op jit(solution)/shard_map/pallas_call | solution.py:583
  32.5 0.0 copy-done.2
  32.5 0.0 copy-done.3
  32.5 0.0 copy-start.4
  32.6 0.0 copy-start.5
  32.6 5.6 %shard_map.129.part = bf16[2048,256]{1,0:T(8,128)(2,1)S(1)} custom-call(s32[192]{0:T(256)S(1)} %bitcast.6, s32[192]{0:T(256)S(1)} %bitcast.8, s32[1]{0:T(128)} %bitcast.4.count_ref, bf16[192,64,64]{2,1,0:T(8,128)(2,1)} %bitcast.10, bf16[4096,256]{1,0:T(8,128)(2,1)S(1)} %shard_map.128.src_ref), custom_call_target="tpu_custom_call" | custom-call | flops 402653184 | bytes 3670016 | tf_op jit(solution)/shard_map/pallas_call | solution.py:61
  38.1 0.0 copy-done.4
  38.1 0.0 copy-done.5
  38.2 30.4 %shard_map.130 = (bf16[512,256]{1,0:T(8,128)(2,1)S(1)}, f32[512,256]{1,0:T(8,128)S(1)}, bf16[2048,256]{1,0:T(8,128)(2,1)S(1)}, bf16[896,1024]{1,0:T(8,128)(2,1)}) custom-call(bf16[2048,256]{1,0:T(8,128)(2,1)S(1)} %shard_map.129.part, bf16[512,256]{1,0:T(8,128)(2,1)S(1)} %copy-done.1, bf16[512,256]{1,0:T(8,128)(2,1)S(1)} %copy-done.5, ...), custom_call_target="tpu_custom_call" | custom-call | flops 5637144576 | bytes 7340032 | tf_op jit(solution)/shard_map/pallas_call | solution.py:237
  68.6 6.5 %shard_map.131.back = bf16[4096,256]{1,0:T(8,128)(2,1)S(1)} custom-call(s32[192]{0:T(256)S(1)} %bitcast.9, s32[192]{0:T(256)S(1)} %bitcast.7, s32[1]{0:T(128)} %bitcast.5.count_ref, bf16[192,64,64]{2,1,0:T(8,128)(2,1)} %bitcast.11, bf16[2048,256]{1,0:T(8,128)(2,1)S(1)} %get-tuple-element.14.src_ref), custom_call_target="tpu_custom_call" | custom-call | flops 402653184 | bytes 5767168 | tf_op jit(solution)/shard_map/pallas_call | solution.py:61
  75.1 0.0 copy-start
  75.1 1.3 copy-done
  76.4 57.8 %shard_map.132 = (bf16[512,256]{1,0:T(8,128)(2,1)S(1)}, bf16[1024,256]{1,0:T(8,128)(2,1)S(1)}, bf16[1024,1024]{1,0:T(8,128)(2,1)}, bf16[512,1024]{1,0:T(8,128)(2,1)S(1)}) custom-call(bf16[4096,256]{1,0:T(8,128)(2,1)} %copy-done, f32[512,256]{1,0:T(8,128)S(1)} %get-tuple-element.15.direct, bf16[896,1024]{1,0:T(8,128)(2,1)} %get-tuple-element.16.g_half), custom_call_target="tpu_custom_call" | custom-call | tf_op jit(solution)/shard_map/pallas_call | solution.py:455
  134.2 4.2 %convert_multiply_fusion = f32[1024,1024]{1,0:T(8,128)} fusion(bf16[1024,1024]{1,0:T(8,128)(2,1)} %get-tuple-element.19), kind=kLoop, calls=%fused_computation | loop fusion | flops 2097152 | bytes 6291456 | tf_op jit(solution)/shard_map/mul | solution.py:619
  138.4 1.6 %convert_multiply_fusion.1 = f32[512,1024]{1,0:T(8,128)} fusion(bf16[512,1024]{1,0:T(8,128)(2,1)S(1)} %get-tuple-element.18), kind=kLoop, calls=%fused_computation.1 | loop fusion | flops 1048576 | bytes 3145728 | tf_op jit(solution)/shard_map/mul | solution.py:618
  140.0 1.0 convert_multiply_fusion.2
  141.0 0.7 copy.18
  141.7 0.7 copy.19
Async XLA Ops:
  0.6 5.8 %copy-start.1 = (bf16[512,256]{1,0:T(8,128)(2,1)S(1)}, bf16[512,256]{1,0:T(8,128)(2,1)}, u32[]{:S(2)}) copy-start(bf16[512,256]{1,0:T(8,128)(2,1)} %feat.3) | copy-start | bytes 786436
  5.8 26.7 %copy-start.2 = (s32[1,1,192]{2,1,0:T(1,128)S(1)}, s32[1,1,192]{2,1,0:T(1,128)}, u32[]{:S(2)}) copy-start(s32[1,1,192]{2,1,0:T(1,128)} %param.12) | copy-start | bytes 2308
  5.8 26.8 %copy-start.3 = (s32[1,1,192]{2,1,0:T(1,128)S(1)}, s32[1,1,192]{2,1,0:T(1,128)}, u32[]{:S(2)}) copy-start(s32[1,1,192]{2,1,0:T(1,128)} %param.11) | copy-start | bytes 2308
  32.5 5.6 %copy-start.4 = (bf16[1024,256]{1,0:T(8,128)(2,1)S(1)}, bf16[1024,256]{1,0:T(8,128)(2,1)}, u32[]{:S(2)}) copy-start(bf16[1024,256]{1,0:T(8,128)(2,1)} %w_out.1) | copy-start | bytes 1572868
  32.6 5.6 %copy-start.5 = (bf16[512,256]{1,0:T(8,128)(2,1)S(1)}, bf16[512,256]{1,0:T(8,128)(2,1)}, u32[]{:S(2)}) copy-start(bf16[512,256]{1,0:T(8,128)(2,1)} %cot.1) | copy-start | bytes 786436
  75.1 1.3 copy-start

commit v3 on v2

--- a/solution.py
+++ b/solution.py
@@ -320,7 +320,9 @@
         )
 
     stage1 = []
-    for q, (at, rows) in enumerate(chunks):
+
+    def over_col(q):
+        at, rows = chunks[q]
         m = rows // 2 // ncol
         copies = []
         for d in range(1, ncol):
@@ -334,6 +336,9 @@
             )
         stage1.append(copies)
 
+    over_col(0)
+    over_col(1)
+
     across = []
 
     def across_send(d):
@@ -360,6 +365,8 @@
         base = at // 2 // ncol
         for copy in stage1[q]:
             copy.wait()
+        if q + 2 < len(chunks):
+            over_col(q + 2)
         value = g_half[rows_at(at // 2 + c * m, m, 16), :].astype(F32)
         for d in range(1, ncol):
             value = value + g_col[d - 1, pl.ds(base, m), :].astype(F32)

time: 143 us -> 145 us (1.014)
  no operation moved by 1% of the time
where the time goes in v3:
time: 145 us; the launch traced here: 143 us
  Pallas kernels  127 us (88%)
  local copies, waits for them, and re-layouts  7.88 us (5%)
  other arithmetic  6.84 us (5%)
    pallas_call x1, Pallas kernels, tail(): pl.pallas_call(functools.partial(tail_kernel, nrow, ncol), out_shape=(sha...  58.8 us
    pallas_call x1, Pallas kernels, middle(): pl.pallas_call(functools.partial(middle_kernel, ncol), out_shape=(shape((...  29.5 us
    pallas_call x1, Pallas kernels, gather(): pl.pallas_call(functools.partial(gather_kernel, nrow), out_shape=jax.Shap...  26 us
    pallas_call x2, Pallas kernels, cell_term(): pl.pallas_call(functools.partial(cell_kernel, transposed), out_shape=jax....  12.6 us
    unnamed x15, local copies, waits for them, and re-layouts  7.88 us
    mul x1, other arithmetic, shards(): sum_mid.astype(F32) * ratio  4.2 us

profile of v3, /device:TPU:0, one launch (start us, length us, event | category | flops | bytes accessed | tf_op | source)
XLA Modules:
  0.0 143.1 jit_solution(8495966005434158505)
XLA Ops:
  0.6 0.0 copy-start.1
  0.6 5.1 %copy.14 = bf16[1,1,192,64,64]{4,3,2,1,0:T(8,128)(2,1)} copy(bf16[1,1,192,64,64]{2,4,3,1,0:T(8,128)(2,1)} %param.10) | data formatting | bytes 3145728 | tf_op args[1]
  5.8 0.0 copy-start.2
  5.8 0.0 copy-start.3
  6.5 0.0 copy-done.1
  6.5 26.0 %shard_map.128.src_ref = bf16[4096,256]{1,0:T(8,128)(2,1)S(1)} custom-call(bf16[512,256]{1,0:T(8,128)(2,1)S(1)} %copy-done.1), custom_call_target="tpu_custom_call" | custom-call | tf_op jit(solution)/shard_map/pallas_call | solution.py:590
  32.5 0.0 copy-done.2
  32.5 0.0 copy-done.3
  32.5 0.0 copy-start.4
  32.6 0.0 copy-start.5
  32.6 5.8 %shard_map.129.part = bf16[2048,256]{1,0:T(8,128)(2,1)S(1)} custom-call(s32[192]{0:T(256)S(1)} %bitcast.6, s32[192]{0:T(256)S(1)} %bitcast.8, s32[1]{0:T(128)} %bitcast.4.count_ref, bf16[192,64,64]{2,1,0:T(8,128)(2,1)} %bitcast.10, bf16[4096,256]{1,0:T(8,128)(2,1)S(1)} %shard_map.128.src_ref), custom_call_target="tpu_custom_call" | custom-call | flops 402653184 | bytes 3670016 | tf_op jit(solution)/shard_map/pallas_call | solution.py:61
  38.4 0.0 copy-done.4
  38.4 0.0 copy-done.5
  38.4 29.5 %shard_map.130 = (bf16[512,256]{1,0:T(8,128)(2,1)S(1)}, f32[512,256]{1,0:T(8,128)S(1)}, bf16[2048,256]{1,0:T(8,128)(2,1)S(1)}, bf16[896,1024]{1,0:T(8,128)(2,1)}) custom-call(bf16[2048,256]{1,0:T(8,128)(2,1)S(1)} %shard_map.129.part, bf16[512,256]{1,0:T(8,128)(2,1)S(1)} %copy-done.1, bf16[512,256]{1,0:T(8,128)(2,1)S(1)} %copy-done.5, ...), custom_call_target="tpu_custom_call" | custom-call | flops 5637144576 | bytes 7340032 | tf_op jit(solution)/shard_map/pallas_call | solution.py:237
  67.9 6.8 %shard_map.131.back = bf16[4096,256]{1,0:T(8,128)(2,1)S(1)} custom-call(s32[192]{0:T(256)S(1)} %bitcast.9, s32[192]{0:T(256)S(1)} %bitcast.7, s32[1]{0:T(128)} %bitcast.5.count_ref, bf16[192,64,64]{2,1,0:T(8,128)(2,1)} %bitcast.11, bf16[2048,256]{1,0:T(8,128)(2,1)S(1)} %get-tuple-element.14.src_ref), custom_call_target="tpu_custom_call" | custom-call | flops 402653184 | bytes 5767168 | tf_op jit(solution)/shard_map/pallas_call | solution.py:61
  74.7 0.0 copy-start
  74.7 1.3 copy-done
  76.0 58.8 %shard_map.132 = (bf16[512,256]{1,0:T(8,128)(2,1)S(1)}, bf16[1024,256]{1,0:T(8,128)(2,1)S(1)}, bf16[1024,1024]{1,0:T(8,128)(2,1)}, bf16[512,1024]{1,0:T(8,128)(2,1)S(1)}) custom-call(bf16[4096,256]{1,0:T(8,128)(2,1)} %copy-done, f32[512,256]{1,0:T(8,128)S(1)} %get-tuple-element.15.direct, bf16[896,1024]{1,0:T(8,128)(2,1)} %get-tuple-element.16.g_half), custom_call_target="tpu_custom_call" | custom-call | tf_op jit(solution)/shard_map/pallas_call | solution.py:462
  134.8 4.2 %convert_multiply_fusion = f32[1024,1024]{1,0:T(8,128)} fusion(bf16[1024,1024]{1,0:T(8,128)(2,1)} %get-tuple-element.19), kind=kLoop, calls=%fused_computation | loop fusion | flops 2097152 | bytes 6291456 | tf_op jit(solution)/shard_map/mul | solution.py:626
  139.0 1.6 %convert_multiply_fusion.1 = f32[512,1024]{1,0:T(8,128)} fusion(bf16[512,1024]{1,0:T(8,128)(2,1)S(1)} %get-tuple-element.18), kind=kLoop, calls=%fused_computation.1 | loop fusion | flops 1048576 | bytes 3145728 | tf_op jit(solution)/shard_map/mul | solution.py:625
  140.6 1.0 convert_multiply_fusion.2
  141.6 0.7 copy.18
  142.3 0.7 copy.19
Async XLA Ops:
  0.6 5.8 %copy-start.1 = (bf16[512,256]{1,0:T(8,128)(2,1)S(1)}, bf16[512,256]{1,0:T(8,128)(2,1)}, u32[]{:S(2)}) copy-start(bf16[512,256]{1,0:T(8,128)(2,1)} %feat.3) | copy-start | bytes 786436
  5.8 26.7 %copy-start.2 = (s32[1,1,192]{2,1,0:T(1,128)S(1)}, s32[1,1,192]{2,1,0:T(1,128)}, u32[]{:S(2)}) copy-start(s32[1,1,192]{2,1,0:T(1,128)} %param.12) | copy-start | bytes 2308
  5.8 26.8 %copy-start.3 = (s32[1,1,192]{2,1,0:T(1,128)S(1)}, s32[1,1,192]{2,1,0:T(1,128)}, u32[]{:S(2)}) copy-start(s32[1,1,192]{2,1,0:T(1,128)} %param.11) | copy-start | bytes 2308
  32.5 5.8 %copy-start.4 = (bf16[1024,256]{1,0:T(8,128)(2,1)S(1)}, bf16[1024,256]{1,0:T(8,128)(2,1)}, u32[]{:S(2)}) copy-start(bf16[1024,256]{1,0:T(8,128)(2,1)} %w_out.1) | copy-start | bytes 1572868
  32.6 5.8 %copy-start.5 = (bf16[512,256]{1,0:T(8,128)(2,1)S(1)}, bf16[512,256]{1,0:T(8,128)(2,1)}, u32[]{:S(2)}) copy-start(bf16[512,256]{1,0:T(8,128)(2,1)} %cot.1) | copy-start | bytes 786436
  74.7 1.3 copy-start
